TPU v7x, 32 devices: a whole 2x2x4 slice. The times are simulated.
32 devices in a mesh: dom: 2 (over x), row: 8 (over z, y), col: 2 (over core).
Axes of the slice: x: 2, y: 2, z: 4, core: 2. Of those that a mesh axis runs over, the one named last changes fastest.
Arguments:
- pair: bfloat16 [224, 112, 128], P(('dom', 'row'), 'col'), parts along dimension 0, may hold values from -6 to 6
- length: int32 [2], P('dom'), parts along dimension 0, may hold values from 56 to 112
- w_tri_in: bfloat16 [128, 640], replicated, may hold values from -0.5 to 0.5
- w_tri_out: bfloat16 [128, 128], replicated, may hold values from -0.5 to 0.5
- w_att: bfloat16 [128, 512], replicated, may hold values from -4 to 4
- w_bias: bfloat16 [128, 4], replicated, may hold values from -0.5 to 0.5
- w_att_out: bfloat16 [128, 128], replicated, may hold values from -0.5 to 0.5
- w_up: bfloat16 [128, 1024], replicated, may hold values from -0.5 to 0.5
- w_down: bfloat16 [512, 128], replicated, may hold values from -0.25 to 0.25
Outputs:
- pair_out: bfloat16 [224, 112, 128], P(('dom', 'row', 'col')), parts along dimension 0
There are 2 independent parts, one for each index of `dom`. A program takes and returns all parts, laid end to end along the dimension named above; an argument that names none is the same for every part. Nothing has to cross between parts.
All inputs are finite; a program needn't handle non-finite values.
Results may differ from a plain program's by a relative error of at most 0.012.
Values may be sent and summed in bfloat16 or wider, within the bound.
A program may use at most 192 MiB of HBM per device.

v0:
```python
import jax
import jax.numpy as jnp
from jax import lax
from jax.sharding import PartitionSpec as P

HEADS = 4


def layer_norm(values_in):
    average = jnp.mean(values_in, axis=-1, keepdims=True)
    centered = values_in - average
    variance = jnp.mean(centered * centered, axis=-1, keepdims=True)
    return centered * lax.rsqrt(variance + 1e-05)


def project(operand, weight):
    flat = operand.reshape(-1, operand.shape[-1])
    product = jnp.dot(flat, weight, preferred_element_type=jnp.float32)
    return product.reshape(operand.shape[:-1] + (weight.shape[1],))


def shards(pair, length, w_tri_in, w_tri_out, w_att, w_bias, w_att_out, w_up, w_down):
    row_count, col_count, channels = pair.shape
    full_length = col_count * lax.axis_size("col")
    head_size = channels // HEADS
    hidden_units = w_down.shape[0]
    row_offset = lax.axis_index("row") * row_count
    col_offset = lax.axis_index("col") * col_count
    valid_length = length[0]
    row_keep = row_offset + jnp.arange(row_count, dtype=jnp.int32) < valid_length
    col_keep = col_offset + jnp.arange(col_count, dtype=jnp.int32) < valid_length
    cell_keep = (row_keep[:, None] & col_keep[None, :]).astype(jnp.float32)[:, :, None]
    residual = pair.astype(jnp.float32)
    normed = layer_norm(residual).astype(jnp.bfloat16)
    projected = project(normed, w_tri_in).reshape(row_count, col_count, 5, channels)
    left_edge = (cell_keep * jax.nn.sigmoid(projected[:, :, 1]) * projected[:, :, 0]).astype(
        jnp.bfloat16
    )
    right_edge = (cell_keep * jax.nn.sigmoid(projected[:, :, 3]) * projected[:, :, 2]).astype(
        jnp.bfloat16
    )
    out_gate = jax.nn.sigmoid(projected[:, :, 4])
    partial_value = jnp.einsum(
        "ikc,jkc->ijc",
        left_edge,
        lax.all_gather(right_edge, "row", axis=0, tiled=True),
        preferred_element_type=jnp.float32,
    )
    summed = lax.psum_scatter(partial_value, "col", scatter_dimension=1, tiled=True)
    tri_norm = layer_norm(summed).astype(jnp.bfloat16)
    after_tri = (residual + out_gate * project(tri_norm, w_tri_out)).astype(jnp.bfloat16)
    slab_pair = lax.all_to_all(after_tri, "col", split_axis=0, concat_axis=1, tiled=True)
    slab_f = slab_pair.astype(jnp.float32)
    slab_rows = slab_pair.shape[0]
    slab_norm = layer_norm(slab_f).astype(jnp.bfloat16)
    slab_bias = jnp.transpose(project(slab_norm, w_bias), (2, 0, 1)).astype(jnp.bfloat16)
    pair_bias = lax.all_gather(slab_bias, ("row", "col"), axis=1, tiled=True)
    bias_float = pair_bias.astype(jnp.float32)
    att_proj = project(slab_norm, w_att).reshape(slab_rows, full_length, 4, channels)
    queries = (
        (att_proj[:, :, 0] * head_size ** (-0.5))
        .astype(jnp.bfloat16)
        .reshape(slab_rows, full_length, HEADS, head_size)
    )
    key_rows = (
        att_proj[:, :, 1].astype(jnp.bfloat16).reshape(slab_rows, full_length, HEADS, head_size)
    )
    values = (
        att_proj[:, :, 2].astype(jnp.bfloat16).reshape(slab_rows, full_length, HEADS, head_size)
    )
    att_gate = jax.nn.sigmoid(att_proj[:, :, 3])
    key_keep = jnp.arange(full_length, dtype=jnp.int32) < valid_length

    def one_row(row_items):
        query_row, key_row, value_row = row_items
        scores = (
            jnp.einsum("jhd,khd->hjk", query_row, key_row, preferred_element_type=jnp.float32)
            + bias_float
        )
        scores = jnp.where(key_keep[None, None, :], scores, jnp.float32(-1000000000.0))
        peak = jnp.max(scores, axis=-1, keepdims=True)
        expo = jnp.exp(scores - peak)
        weights = (expo / jnp.sum(expo, axis=-1, keepdims=True)).astype(jnp.bfloat16)
        mixed = jnp.einsum("hjk,khd->jhd", weights, value_row, preferred_element_type=jnp.float32)
        return mixed.reshape(full_length, channels)

    attended = lax.map(one_row, (queries, key_rows, values))
    gated_out = (att_gate * attended).astype(jnp.bfloat16)
    second = (slab_f + project(gated_out, w_att_out)).astype(jnp.bfloat16)
    second_f = second.astype(jnp.float32)
    hidden = project(layer_norm(second_f).astype(jnp.bfloat16), w_up)
    activated = (jax.nn.silu(hidden[..., :hidden_units]) * hidden[..., hidden_units:]).astype(
        jnp.bfloat16
    )
    return (second_f + project(activated, w_down)).astype(jnp.bfloat16)


def solution(mesh):
    placed = (P(("dom", "row"), "col", None), P("dom"), P(), P(), P(), P(), P(), P(), P())
    return jax.shard_map(
        shards,
        mesh=mesh,
        in_specs=placed,
        out_specs=P(("dom", "row", "col"), None, None),
        check_vma=False,
    )
```

profile of v0, /device:TPU:0, one launch (start us, length us, event | category | flops | bytes accessed | tf_op | source)
XLA Modules:
  0.0 139.5 jit_solution(2213114445478987624)
XLA Ops:
  7.2 1.1 convert_reduce_fusion
  8.4 1.3 fusion.30
  9.6 1.1 copy.91
  10.8 1.6 %fusion.67 = f32[14,56,5,128]{3,1,2,0:T(8,128)S(1)} fusion(bf16[5,128,128,1]{2,1,0,3:T(8,128)(2,1)S(1)} %bitcast.197, bf16[14,56,128]{2,1,0:T(8,128)(2,1)} %param.11, f32[14,56]{1,0:T(8,128)S(1)} %add_rsqrt_fusion.2, f32[14,56]{1,0:T(8,128)S(1)} %broadcast_multiply_fusion.2), kind=kOutput, calls=%fused_computation.87 | convolution fusion | flops 128851968 | bytes 2377856 | tf_op jit(solution)/shard_map/dot_general | solution.py:18
  12.4 0.9 fusion.39
  13.4 1.2 copy.97
  14.6 45.9 %all-gather.2.cloned.1.call-done = bf16[112,56,128]{2,1,0:T(8,128)(2,1)} async-done(((bf16[14,56,128]{2,1,0:T(8,128)(2,1)}), bf16[112,56,128]{2,1,0:T(8,128)(2,1)}) %all-gather.2.cloned.1.call-update) | async-done | bytes 1605648 | tf_op jit(solution)/shard_map/all_gather | solution.py:46
  60.5 7.2 %copy.96 = bf16[112,56,128]{1,0,2:T(8,128)(2,1)} copy(bf16[112,56,128]{2,1,0:T(8,128)(2,1)} %all-gather.2.cloned.1.call-done) | data formatting | bytes 3211264 | tf_op jit(solution)/shard_map/all_gather | solution.py:46
  67.7 4.1 %convolution_bitcast_fusion = f32[14,112,128]{1,0,2:T(8,128)S(1)} fusion(bf16[112,56,128]{1,0,2:T(8,128)(2,1)} %copy.96, bf16[14,56,128]{1,0,2:T(8,128)(2,1)} %copy.97), kind=kOutput, calls=%fused_computation.21 | convolution fusion | flops 22478848 | bytes 2609152 | tf_op jit(solution)/shard_map/ikc,jkc->ijc/dot_general | solution.py:43
  71.8 1.6 %copy.98 = f32[14,112,128]{2,0,1:T(8,128)} copy(f32[14,112,128]{1,0,2:T(8,128)S(1)} %convolution_bitcast_fusion) | data formatting | bytes 1605632 | tf_op jit(solution)/shard_map/ikc,jkc->ijc/transpose | solution.py:43
  73.6 7.2 %reduce-scatter.2.cloned.1.call-done = f32[14,56,128]{2,0,1:T(8,128)} async-done(((f32[14,112,128]{2,0,1:T(8,128)}), f32[14,56,128]{2,0,1:T(8,128)}) %reduce-scatter.2.cloned.1.call-update) | async-done | bytes 401424 | tf_op jit(solution)/shard_map/reduce_scatter | solution.py:49
  80.8 1.2 reduce_sum.83
  82.2 1.4 multiply_reduce_fusion
  83.7 1.3 multiply_convert_fusion
  85.4 3.9 %all_to_all.4 = bf16[14,56,128]{2,1,0:T(8,128)(2,1)S(1)} all-to-all(bf16[14,56,128]{2,1,0:T(8,128)(2,1)S(1)} %fusion.25), channel_id=1, replica_groups=mesh['dom'=2,'row'=8,'col'=2] {'col'}, dimensions={0} | all-to-all | bytes 401408 | tf_op jit(solution)/shard_map/all_to_all | solution.py:52
  90.8 21.9 %all_gather.7 = bf16[4,112,112]{2,0,1:T(4,128)(2,1)S(1)} all-gather(bf16[4,7,112]{2,0,1:T(4,128)(2,1)S(1)} %fusion.26), channel_id=1, replica_groups=mesh['dom'=2,'row'=8,'col'=2] {'row','col'}, dimensions={1}, use_global_device_ids=true | all-gather | bytes 106624 | tf_op jit(solution)/shard_map/all_gather | solution.py:57
  113.9 14.8 %while.11 = (s32[]{:T(128)}, f32[7,112,128]{2,1,0:T(8,128)}, bf16[7,112,4,32]{1,3,2,0:T(8,128)(2,1)S(1)}, bf16[7,112,4,32]{1,3,2,0:T(8,128)(2,1)S(1)}, bf16[7,11...) while((s32[]{:T(128)}, f32[7,112,128]{2,1,0:T(8,128)}, ...), condition=%wide.region_10.11_spmd.clone, body=%wide.region_7.10_spmd.clone.sunk | while | flops 10086160 | bytes 1576397 | solution.py:87
  113.9 0.7 iota_compare_fusion.2
  115.4 0.6 constant_dynamic-update-slice_fusion.2
  116.0 0.6 iota_compare_fusion.2
  117.5 0.6 constant_dynamic-update-slice_fusion.2
  118.1 0.6 iota_compare_fusion.2
  119.6 0.6 constant_dynamic-update-slice_fusion.2
  120.3 0.6 iota_compare_fusion.2
  121.8 0.6 constant_dynamic-update-slice_fusion.2
  122.4 0.6 iota_compare_fusion.2
  124.5 0.6 iota_compare_fusion.2
  126.6 0.6 iota_compare_fusion.2
  128.1 0.6 constant_dynamic-update-slice_fusion.2
  128.7 1.4 fusion.88
  130.5 0.6 fusion.63
  131.4 1.3 fusion.22
  (86 shorter events, 11.1 us)
Async XLA Ops:
  6.5 124.0 %copy-start = (bf16[128,1024]{1,0:T(8,128)(2,1)S(1)}, bf16[128,1024]{1,0:T(8,128)(2,1)}, u32[]{:S(2)}) copy-start(bf16[128,1024]{1,0:T(8,128)(2,1)} %param.18) | copy-start | bytes 786436
  6.5 53.9 %all-gather.2.cloned.1.call-start = ((), (), s32[]{:S(2)}) async-start(), calls=%async_computation.2 | async-start | bytes 1806336 | tf_op jit(solution)/shard_map/all_gather | solution.py:46
  13.3 67.5 %reduce-scatter.2.cloned.1.call-start = ((), (), s32[]{:S(2)}) async-start(), calls=%async_computation.3 | async-start | bytes 1376256 | tf_op jit(solution)/shard_map/reduce_scatter | solution.py:49
  71.8 1.6 %copy-start.2 = (bf16[128,512]{1,0:T(8,128)(2,1)S(1)}, bf16[128,512]{1,0:T(8,128)(2,1)}, u32[]{:S(2)}) copy-start(bf16[128,512]{1,0:T(8,128)(2,1)} %param.15) | copy-start | bytes 393220
  73.4 11.7 %copy-start.1 = (bf16[14,56,128]{2,1,0:T(8,128)(2,1)S(1)}, bf16[14,56,128]{2,1,0:T(8,128)(2,1)}, u32[]{:S(2)}) copy-start(bf16[14,56,128]{2,1,0:T(8,128)(2,1)} %param.11) | copy-start | bytes 602116
  73.4 11.7 %copy-start.5 = (bf16[128,128]{1,0:T(8,128)(2,1)S(1)}, bf16[128,128]{1,0:T(8,128)(2,1)}, u32[]{:S(2)}) copy-start(bf16[128,128]{1,0:T(8,128)(2,1)} %param.14) | copy-start | bytes 98308
  85.4 5.2 %copy-start.3 = (bf16[128,4]{0,1:T(4,128)(2,1)S(1)}, bf16[128,4]{0,1:T(4,128)(2,1)}, u32[]{:S(2)}) copy-start(bf16[128,4]{0,1:T(4,128)(2,1)} %param.16) | copy-start | bytes 3076
  113.9 14.8 %copy-start.6 = (bf16[128,128]{1,0:T(8,128)(2,1)S(1)}, bf16[128,128]{1,0:T(8,128)(2,1)}, u32[]{:S(2)}) copy-start(bf16[128,128]{1,0:T(8,128)(2,1)} %param.17) | copy-start | bytes 98308
  130.5 0.9 copy-start.4
Sparse Core Ops, SparseCore 0:
  13.4 46.9 all-gather.1
  73.6 7.1 reduce-scatter.1
where the time goes:
time: 140 us
  waiting for transfers between devices  53.1 us (38%)
  blocking collectives  25.8 us (18%)
  local copies, waits for them, and re-layouts  17.7 us (13%)
  matrix products  14.9 us (11%)
  between operations  14.4 us (10%)
  other arithmetic  13.3 us (10%)
    all_gather x1, waiting for transfers between devices, shards(): lax.all_gather(right_edge, 'row', axis=0, tiled=True)  45.9 us
    all_gather x1, blocking collectives, shards(): pair_bias = lax.all_gather(slab_bias, ('row', 'col'), axis=1, tiled=True)  21.9 us
    all_gather x1, local copies, waits for them, and re-layouts, shards(): lax.all_gather(right_edge, 'row', axis=0, tiled=True)  7.22 us
    reduce_scatter x1, waiting for transfers between devices, shards(): lax.psum_scatter(partial_value, 'col', scatter_dimension=1, tiled=True)  7.22 us
    dot_general x7, matrix products, project(): product = jnp.dot(flat, weight, preferred_element_type=jnp.float32)  5.67 us
    dynamic_update_slice x14, local copies, waits for them, and re-layouts, shards(): attended = lax.map(one_row, (queries, key_rows, values))  5.02 us
    lt x7, other arithmetic, shards(): key_keep = jnp.arange(full_length, dtype=jnp.int32) < valid_length  4.55 us
    dot_general x1, matrix products, shards(): jnp.einsum('ikc,jkc->ijc', left_edge, lax.all_gather(right_edge, 'row', a...  4.14 us
  transfers between devices with their start and end apart: 2, of which 2 were waited for; matrix products, arithmetic and copies ran while one was open for 1% of the time, Pallas kernels for 0%

commit v1 on v0

v1 whole, which is shorter than its diff:
```python
import functools

import jax
import jax.numpy as jnp
from jax import lax
from jax.experimental import pallas as pl
from jax.experimental.pallas import tpu as pltpu
from jax.sharding import PartitionSpec as P

HEADS = 4
F32 = jnp.float32
BF16 = jnp.bfloat16
MESH = pl.DeviceIdType.MESH


def layer_norm(values_in):
    average = jnp.mean(values_in, axis=-1, keepdims=True)
    centered = values_in - average
    variance = jnp.mean(centered * centered, axis=-1, keepdims=True)
    return centered * lax.rsqrt(variance + 1e-05)


def mul(left, right):
    return jnp.dot(left, right, preferred_element_type=F32)


def mul_t(left, right):
    return lax.dot_general(left, right, (((1,), (1,)), ((), ())), preferred_element_type=F32)


def kernel(
    rows_n,
    length_ref,
    pair_ref,
    w_tri_in,
    w_tri_out,
    w_att,
    w_bias,
    w_att_out,
    w_up,
    w_down,
    out_ref,
    normed,
    right_all,
    left_f,
    pair_other,
    gate,
    acc,
    part_out,
    part_in,
    after,
    slab,
    keys_s,
    values_s,
    queries_s,
    att_gate,
    bias_own,
    bias_all,
    bias_f,
    ring_send,
    ring_recv,
    part_send,
    part_recv,
    pair_send,
    pair_recv,
    bias_send,
    bias_recv,
):
    rows, cols, channels = pair_ref.shape
    full = 2 * cols
    padded = slab.shape[1]
    slab_rows = rows // 2
    hidden_units = w_down.shape[0]
    head_size = channels // HEADS
    peers = 2 * rows_n
    half_ring = rows_n // 2
    pair_cells = 2 * cols
    cells = rows * cols
    first_pairs = (rows + 2) // 4
    parts = ((0, first_pairs), (first_pairs, rows // 2 - first_pairs))
    snake = rows_n <= 8

    row = lax.axis_index("row")
    col = lax.axis_index("col")
    me = row * 2 + col

    def place(r):
        if not snake:
            return r
        return jnp.where(r % 2 == 0, r // 2, rows_n - 1 - r // 2)

    def owner_at(p):
        p = lax.rem(p + 2 * rows_n, rows_n)
        if not snake:
            return p
        return jnp.where(p < rows_n // 2, 2 * p, 2 * (rows_n - p) - 1)

    pos = place(row)
    nexts = (owner_at(pos + 1), owner_at(pos - 1))

    barrier = pltpu.get_barrier_semaphore()

    def greet(t, carry):
        peer = lax.rem(me + t, peers)
        pl.semaphore_signal(
            barrier, inc=1, device_id={"row": peer // 2, "col": peer % 2}, device_id_type=MESH
        )
        return carry

    lax.fori_loop(1, peers, greet, 0)

    length = length_ref[0]
    row_off = row * rows
    col_off = col * cols
    flat = lax.broadcasted_iota(jnp.int32, (pair_cells, channels), 0)
    second_row = (flat >= cols).astype(jnp.int32)
    col_ok = col_off + flat - cols * second_row < length

    def keep_of(p):
        return col_ok & (row_off + 2 * p + second_row < length)

    def right_step(p, carry):
        block = pair_ref[pl.ds(2 * p, 2)].astype(F32).reshape(pair_cells, channels)
        norm = layer_norm(block).astype(BF16)
        at = pl.ds(pl.multiple_of(p * pair_cells, 16), pair_cells)
        normed[at, :] = norm
        proj = mul(norm, w_tri_in[:, 2 * channels : 4 * channels])
        edge = jax.nn.sigmoid(proj[:, channels:]) * proj[:, :channels]
        to = pl.ds(pl.multiple_of(row * cells + p * pair_cells, 16), pair_cells)
        right_all[to, :] = jnp.where(keep_of(p), edge, 0.0).astype(BF16)
        return carry

    def ring_copy(way, dist, part, owner):
        start, count = parts[part]
        at = pl.ds(
            pl.multiple_of(owner * cells + start * pair_cells, 16), count * pair_cells
        )
        return pltpu.make_async_remote_copy(
            src_ref=right_all.at[at],
            dst_ref=right_all.at[at],
            send_sem=ring_send.at[way, dist, part],
            recv_sem=ring_recv.at[way, dist, part],
            device_id={"row": nexts[way]},
            device_id_type=MESH,
        )

    pair_copy = pltpu.make_async_remote_copy(
        src_ref=pair_ref.at[pl.ds((1 - col) * slab_rows, slab_rows)],
        dst_ref=pair_other,
        send_sem=pair_send,
        recv_sem=pair_recv,
        device_id={"col": 1 - col},
        device_id_type=MESH,
    )

    lax.fori_loop(0, first_pairs, right_step, 0)
    pl.semaphore_wait(barrier, peers - 1)
    ring_copy(0, 1, 0, row).start()
    ring_copy(1, 1, 0, row).start()
    pair_copy.start()
    lax.fori_loop(first_pairs, rows // 2, right_step, 0)
    ring_copy(0, 1, 1, row).start()
    ring_copy(1, 1, 1, row).start()

    def left_step(p, carry):
        at = pl.ds(pl.multiple_of(p * pair_cells, 16), pair_cells)
        proj = mul(normed[at, :], w_tri_in[:, : 2 * channels])
        edge = jax.nn.sigmoid(proj[:, channels:]) * proj[:, :channels]
        edge = jnp.where(keep_of(p), edge, 0.0).astype(BF16).astype(F32)
        left_f[pl.ds(2 * p, 2)] = edge.reshape(2, cols, channels)
        return carry

    lax.fori_loop(0, rows // 2, left_step, 0)

    def part_copy(part, owner):
        start, count = parts[part]
        at = pl.ds(pl.multiple_of((owner * rows + 2 * start) * 8, 16), 16 * count)
        return pltpu.make_async_remote_copy(
            src_ref=part_out.at[at],
            dst_ref=part_in.at[at],
            send_sem=part_send.at[owner, part],
            recv_sem=part_recv.at[owner, part],
            device_id={"col": 1 - col},
            device_id_type=MESH,
        )

    def tri_part(part, owner):
        start, count = parts[part]

        def step(p, carry):
            at = pl.ds(pl.multiple_of(owner * cells + p * pair_cells, 16), pair_cells)
            both = right_all[at, :].astype(F32).reshape(2, cols, channels)
            for side, ref in ((1 - col, part_out), (col, acc)):
                block = left_f[pl.ds(side * slab_rows, slab_rows)]
                for t in range(2):
                    total = jnp.sum(block * both[t][None], axis=1)
                    to = pl.multiple_of((owner * rows + 2 * p + t) * 8, 8)
                    ref[pl.ds(to, slab_rows), :] = total
            return carry

        lax.fori_loop(start, start + count, step, 0)
        part_copy(part, owner).start()

    tri_part(0, row)
    tri_part(1, row)

    pair_copy.wait_recv()

    def whole_row(i):
        own = pair_ref[col * slab_rows + i].astype(F32)
        other = pair_other[i].astype(F32)
        low = jnp.where(col == 0, own, other)
        high = jnp.where(col == 0, other, own)
        return jnp.concatenate([low, high], axis=0)

    def gate_step(i, carry):
        whole = whole_row(i)
        after[i] = whole
        norm = layer_norm(whole).astype(BF16)
        gate[i] = jax.nn.sigmoid(mul(norm, w_tri_in[:, 4 * channels :]))
        return carry

    lax.fori_loop(0, slab_rows, gate_step, 0)

    def ring_step(s, carry):
        owners = (owner_at(pos - s), owner_at(pos + s))
        for part in range(2):
            for way in range(2):
                ring_copy(way, s, part, owners[way]).wait_recv()
                if part == way:
                    ring_copy(way, s + 1, part, owners[way]).start()
                else:

                    @pl.when(s < half_ring - 1)
                    def _():
                        ring_copy(way, s + 1, part, owners[way]).start()

            tri_part(part, owners[0])
            tri_part(part, owners[1])
        return carry

    lax.fori_loop(1, half_ring, ring_step, 0)
    far = owner_at(pos + half_ring)
    for part in range(2):
        ring_copy(part, half_ring, part, far).wait_recv()
        tri_part(part, far)

    def part_wait(owner, carry):
        for part in range(2):
            part_copy(part, owner).wait_recv()
        return carry

    lax.fori_loop(0, rows_n, part_wait, 0)

    bias_own[...] = jnp.zeros_like(bias_own)

    def norm_step(i, carry):
        at = pl.ds(i, full, stride=8)
        summed = acc[at, :] + part_in[at, :]
        tri_norm = layer_norm(summed).astype(BF16)
        fresh = after[i] + gate[i] * mul(tri_norm, w_tri_out[...])
        fresh = fresh.astype(BF16).astype(F32)
        after[i] = fresh
        norm = layer_norm(fresh)
        if padded > full:
            norm = jnp.concatenate([norm, jnp.zeros((padded - full, channels), F32)], axis=0)
        norm = norm.astype(BF16)
        slab[i] = norm
        bias = mul_t(w_bias[...], norm)
        for h in range(HEADS):
            bias_own[pl.ds(8 * h + i, 1), :] = bias[h : h + 1]
        return carry

    lax.fori_loop(0, slab_rows, norm_step, 0)
    bias_all[me] = bias_own[...].astype(BF16)

    def bias_copy(t):
        peer = lax.rem(me + t, peers)
        return pltpu.make_async_remote_copy(
            src_ref=bias_all.at[me],
            dst_ref=bias_all.at[me],
            send_sem=bias_send.at[t],
            recv_sem=bias_recv.at[t],
            device_id={"row": peer // 2, "col": peer % 2},
            device_id_type=MESH,
        )

    def bias_arrival(t):
        peer = lax.rem(me + peers - t, peers)
        return pltpu.make_async_remote_copy(
            src_ref=bias_all.at[peer],
            dst_ref=bias_all.at[peer],
            send_sem=bias_send.at[t],
            recv_sem=bias_recv.at[t],
            device_id={"row": peer // 2, "col": peer % 2},
            device_id_type=MESH,
        )

    def bias_start(t, carry):
        bias_copy(t).start()
        return carry

    lax.fori_loop(1, peers, bias_start, 0)

    head_of = lax.broadcasted_iota(jnp.int32, (full, channels), 1) // head_size

    def att_step(i, carry):
        proj = mul(slab[i], w_att[...])
        queries_s[i] = (proj[:full, :channels] * head_size ** (-0.5)).astype(BF16)
        keys_s[i] = proj[:, channels : 2 * channels].astype(BF16)
        values_s[i, :, :channels] = proj[:, 2 * channels : 3 * channels].astype(BF16)
        values_s[i, :, channels:] = jnp.ones((padded, channels), BF16)
        att_gate[i] = jax.nn.sigmoid(proj[:full, 3 * channels :])
        return carry

    lax.fori_loop(0, slab_rows, att_step, 0)

    def bias_wait(t, carry):
        bias_arrival(t).wait_recv()
        return carry

    lax.fori_loop(1, peers, bias_wait, 0)
    key_ok = lax.broadcasted_iota(jnp.int32, (slab_rows, padded), 1) < length
    for peer in range(peers):
        block = bias_all[peer].astype(F32)
        for h in range(HEADS):
            bias_f[h, peer * slab_rows : (peer + 1) * slab_rows, :] = jnp.where(
                key_ok, block[8 * h : 8 * h + slab_rows], -1000000000.0
            )

    def row_step(i, carry):
        query = queries_s[i].astype(F32)
        key = keys_s[i]
        value = values_s[i]
        top = jnp.zeros((full, channels), F32)
        bottom = jnp.zeros((full, channels), F32)
        for h in range(HEADS):
            mine = head_of == h
            scores = mul_t(jnp.where(mine, query, 0.0).astype(BF16), key) + bias_f[h]
            peak = jnp.max(scores, axis=-1, keepdims=True)
            expo = jnp.exp(scores - peak).astype(BF16)
            mixed = mul(expo, value)
            top = jnp.where(mine, mixed[:, :channels], top)
            bottom = jnp.where(mine, mixed[:, channels:], bottom)
        gated = (att_gate[i] * (top / bottom)).astype(BF16)
        second = (after[i] + mul(gated, w_att_out[...])).astype(BF16).astype(F32)
        hidden = mul(layer_norm(second).astype(BF16), w_up[...])
        activated = jax.nn.silu(hidden[:, :hidden_units]) * hidden[:, hidden_units:]
        result = second + mul(activated.astype(BF16), w_down[...])
        out_ref[i] = result.astype(BF16)
        return carry

    lax.fori_loop(0, slab_rows, row_step, 0)

    pair_copy.wait_send()

    def ring_drain(s, carry):
        owners = (owner_at(pos - s), owner_at(pos + s))
        for way in range(2):
            for part in range(2):
                ring_copy(way, s + 1, part, owners[way]).wait_send()
        return carry

    lax.fori_loop(0, half_ring - 1, ring_drain, 0)
    ring_copy(0, half_ring, 0, owner_at(pos - half_ring + 1)).wait_send()
    ring_copy(1, half_ring, 1, owner_at(pos + half_ring - 1)).wait_send()

    def part_drain(owner, carry):
        for part in range(2):
            part_copy(part, owner).wait_send()
        return carry

    lax.fori_loop(0, rows_n, part_drain, 0)

    def bias_drain(t, carry):
        bias_copy(t).wait_send()
        return carry

    lax.fori_loop(1, peers, bias_drain, 0)


def shards(rows_n, pair, length, w_tri_in, w_tri_out, w_att, w_bias, w_att_out, w_up, w_down):
    rows, cols, channels = pair.shape
    full = 2 * cols
    padded = -(-full // 128) * 128
    slab_rows = rows // 2
    peers = 2 * rows_n
    half_ring = rows_n // 2
    bias_t = jnp.pad(w_bias.T, ((0, 16 - HEADS), (0, 0)))
    vmem = pl.BlockSpec(memory_space=pltpu.VMEM)
    dma = pltpu.SemaphoreType.DMA
    return pl.pallas_call(
        functools.partial(kernel, rows_n),
        out_shape=jax.ShapeDtypeStruct((slab_rows, full, channels), BF16),
        in_specs=[pl.BlockSpec(memory_space=pltpu.SMEM)] + [vmem] * 8,
        out_specs=vmem,
        scratch_shapes=[
            pltpu.VMEM((rows * cols, channels), BF16),
            pltpu.VMEM((rows_n * rows * cols, channels), BF16),
            pltpu.VMEM((rows, cols, channels), F32),
            pltpu.VMEM((slab_rows, cols, channels), BF16),
            pltpu.VMEM((slab_rows, full, channels), F32),
            pltpu.VMEM((full * 8, channels), F32),
            pltpu.VMEM((full * 8, channels), F32),
            pltpu.VMEM((full * 8, channels), F32),
            pltpu.VMEM((slab_rows, full, channels), F32),
            pltpu.VMEM((slab_rows, padded, channels), BF16),
            pltpu.VMEM((slab_rows, padded, channels), BF16),
            pltpu.VMEM((slab_rows, padded, 2 * channels), BF16),
            pltpu.VMEM((slab_rows, full, channels), BF16),
            pltpu.VMEM((slab_rows, full, channels), F32),
            pltpu.VMEM((HEADS * 8, padded), F32),
            pltpu.VMEM((peers, HEADS * 8, padded), BF16),
            pltpu.VMEM((HEADS, full, padded), F32),
            dma((2, half_ring + 1, 2)),
            dma((2, half_ring + 1, 2)),
            dma((rows_n, 2)),
            dma((rows_n, 2)),
            dma,
            dma,
            dma((peers,)),
            dma((peers,)),
        ],
        compiler_params=pltpu.CompilerParams(
            collective_id=0, has_side_effects=True, vmem_limit_bytes=60 * 2**20
        ),
    )(length, pair, w_tri_in, w_tri_out, w_att, bias_t, w_att_out, w_up, w_down)


def solution(mesh):
    placed = (P(("dom", "row"), "col", None), P("dom"), P(), P(), P(), P(), P(), P(), P())
    return jax.shard_map(
        functools.partial(shards, mesh.shape["row"]),
        mesh=mesh,
        in_specs=placed,
        out_specs=P(("dom", "row", "col"), None, None),
        check_vma=False,
    )
```

time: 140 us -> 50.3 us (0.36)
  waiting for transfers between devices: 53.1 us -> 0 us
  Pallas kernels: 0 us -> 46.6 us
  blocking collectives: 25.8 us -> 0 us
  matrix products: 14.9 us -> 0 us
  local copies, waits for them, and re-layouts: 17.7 us -> 2.89 us
  between operations: 14.4 us -> 0.67 us
  other arithmetic: 13.3 us -> 0 us
    pallas_call x0 -> x1, Pallas kernels: none -> 46.6 us  [shards(): pl.pallas_call(functools.partial(kernel, rows_n), out_shape=jax.ShapeDtyp...]
    all_gather x1 -> x0, waiting for transfers between devices: 45.9 us -> none  [shards(): lax.all_gather(right_edge, 'row', axis=0, tiled=True)]
    all_gather x1 -> x0, blocking collectives: 21.9 us -> none  [shards(): pair_bias = lax.all_gather(slab_bias, ('row', 'col'), axis=1, tiled=True)]
    dot_general x22 -> x0, matrix products: 12.8 us -> none  [the longest x7 5.67 us: project(): product = jnp.dot(flat, weight, preferred_element_type=jnp.float32)]
    all_gather x1 -> x0, local copies, waits for them, and re-layouts: 7.22 us -> none  [shards(): lax.all_gather(right_edge, 'row', axis=0, tiled=True)]
    reduce_scatter x1 -> x0, waiting for transfers between devices: 7.22 us -> none  [shards(): lax.psum_scatter(partial_value, 'col', scatter_dimension=1, tiled=True)]
    reduce_sum x7 -> x0, other arithmetic: 5.78 us -> none  [the longest x4 3.29 us: layer_norm(): variance = jnp.mean(centered * centered, axis=-1, keepdims=True)]
    dynamic_update_slice x14 -> x0, local copies, waits for them, and re-layouts: 5.02 us -> none  [shards(): attended = lax.map(one_row, (queries, key_rows, values))]
  transfers between devices with their start and end apart: 2 -> 0, of which waited for: 2 -> 0; matrix products, arithmetic and copies ran while one was open for 1% -> 0% of each run, Pallas kernels for 0% -> 0%
where the time goes in v1:
time: 50.3 us; the launch traced here: 50.2 us
  Pallas kernels  46.6 us (93%)
  local copies, waits for them, and re-layouts  2.89 us (6%)
  between operations  0.67 us (1%)
    pallas_call x1, Pallas kernels, shards(): pl.pallas_call(functools.partial(kernel, rows_n), out_shape=jax.ShapeDtyp...  46.6 us
    unnamed x3, local copies, waits for them, and re-layouts  2.29 us

profile of v1, /device:TPU:0, one launch (start us, length us, event | category | flops | bytes accessed | tf_op | source)
XLA Modules:
  0.0 50.2 jit_solution(14115100686522772123)
XLA Ops:
  0.7 0.0 copy-start
  0.7 0.7 %copy-done = bf16[128,4]{0,1:T(4,128)(2,1)S(1)} copy-done((bf16[128,4]{0,1:T(4,128)(2,1)S(1)}, bf16[128,4]{0,1:T(4,128)(2,1)}, u32[]{:S(2)}) %copy-start) | copy-done | bytes 1048
  1.3 0.6 %pad.4.w_bias = bf16[16,128]{1,0:T(8,128)(2,1)} pad(bf16[4,128]{1,0:T(4,128)(2,1)S(1)} %bitcast.1, bf16[]{:T(256)} %constant.2.clone.1), padding=0_12x0_0 | pad | bytes 5122 | tf_op jit(solution)/shard_map/jit(_pad)/pad | solution.py:389
  1.9 46.6 %shard_map.91 = bf16[7,112,128]{2,1,0:T(8,128)(2,1)} custom-call(s32[1]{0:T(128)S(6)} %copy.11.length_ref, bf16[14,56,128]{2,1,0:T(8,128)(2,1)} %pair_ref.1, bf16[128,640]{1,0:T(8,128)(2,1)} %w_tri_in.1, bf16[128,128]{1,0:T(8,128)(2,1)} %w_tri_out.1, bf16[128,512]{1,0:T(8,128)(2,1)} %w_att.1, bf16[16,128]{1,0:T(8,128)(2,1)} %pad.4.w_bias, ...), custom_call_target="tpu_custom_call" | custom-call | tf_op jit(solution)/shard_map/pallas_call | solution.py:392
  48.5 1.6 %copy.12 = bf16[7,112,128]{2,1,0:T(8,128)(2,1)} copy(bf16[7,112,128]{2,1,0:T(8,128)(2,1)} %shard_map.91) | data formatting | bytes 401408
Async XLA Ops:
  0.7 0.7 %copy-start = (bf16[128,4]{0,1:T(4,128)(2,1)S(1)}, bf16[128,4]{0,1:T(4,128)(2,1)}, u32[]{:S(2)}) copy-start(bf16[128,4]{0,1:T(4,128)(2,1)} %param.14) | copy-start | bytes 3076

commit v2 on v1

--- a/solution.py
+++ b/solution.py
@@ -48,7 +48,8 @@
     acc,
     part_out,
     part_in,
-    after,
+    cells_f,
+    scores_s,
     slab,
     keys_s,
     values_s,
@@ -76,9 +77,16 @@
     half_ring = rows_n // 2
     pair_cells = 2 * cols
     cells = rows * cols
-    first_pairs = (rows + 2) // 4
-    parts = ((0, first_pairs), (first_pairs, rows // 2 - first_pairs))
+    pairs = rows // 2
+    cuts = [0, (pairs + 2) // 4, (pairs + 1) // 2, (3 * pairs + 3) // 4, pairs]
+    parts = tuple((a, b - a) for a, b in zip(cuts[:-1], cuts[1:]))
+    orders = ((0, 1, 2, 3), (2, 3, 0, 1))
+    early = scores_s.shape[1] == full
     snake = rows_n <= 8
+
+    def loop(count, step):
+        lax.fori_loop(0, count, step, 0, unroll=early)
+
 
     row = lax.axis_index("row")
     col = lax.axis_index("col")
@@ -99,15 +107,11 @@
     nexts = (owner_at(pos + 1), owner_at(pos - 1))
 
     barrier = pltpu.get_barrier_semaphore()
-
-    def greet(t, carry):
-        peer = lax.rem(me + t, peers)
+    for way in range(2):
         pl.semaphore_signal(
-            barrier, inc=1, device_id={"row": peer // 2, "col": peer % 2}, device_id_type=MESH
-        )
-        return carry
-
-    lax.fori_loop(1, peers, greet, 0)
+            barrier, inc=1, device_id={"row": nexts[way]}, device_id_type=MESH
+        )
+    pl.semaphore_signal(barrier, inc=1, device_id={"col": 1 - col}, device_id_type=MESH)
 
     length = length_ref[0]
     row_off = row * rows
@@ -153,14 +157,12 @@
         device_id_type=MESH,
     )
 
-    lax.fori_loop(0, first_pairs, right_step, 0)
-    pl.semaphore_wait(barrier, peers - 1)
-    ring_copy(0, 1, 0, row).start()
-    ring_copy(1, 1, 0, row).start()
+    lax.fori_loop(0, pairs, right_step, 0)
+    pl.semaphore_wait(barrier, 3)
+    for turn in range(4):
+        for way in range(2):
+            ring_copy(way, 1, orders[way][turn], row).start()
     pair_copy.start()
-    lax.fori_loop(first_pairs, rows // 2, right_step, 0)
-    ring_copy(0, 1, 1, row).start()
-    ring_copy(1, 1, 1, row).start()
 
     def left_step(p, carry):
         at = pl.ds(pl.multiple_of(p * pair_cells, 16), pair_cells)
@@ -201,8 +203,8 @@
         lax.fori_loop(start, start + count, step, 0)
         part_copy(part, owner).start()
 
-    tri_part(0, row)
-    tri_part(1, row)
+    for part in range(4):
+        tri_part(part, row)
 
     pair_copy.wait_recv()
 
@@ -215,19 +217,31 @@
 
     def gate_step(i, carry):
         whole = whole_row(i)
-        after[i] = whole
+        at = pl.ds(i, full, stride=8)
+        cells_f[at, :] = whole
         norm = layer_norm(whole).astype(BF16)
-        gate[i] = jax.nn.sigmoid(mul(norm, w_tri_in[:, 4 * channels :]))
+        gate[at, :] = jax.nn.sigmoid(mul(norm, w_tri_in[:, 4 * channels :]))
         return carry
 
     lax.fori_loop(0, slab_rows, gate_step, 0)
+
+    def finish(owner):
+        for part in range(4):
+            part_copy(part, owner).wait_recv()
+        at = pl.ds(pl.multiple_of(owner * rows * 8, 16), rows * 8)
+        tri_norm = layer_norm(acc[at, :] + part_in[at, :]).astype(BF16)
+        fresh = cells_f[at, :] + gate[at, :] * mul(tri_norm, w_tri_out[...])
+        fresh = fresh.astype(BF16).astype(F32)
+        acc[at, :] = fresh
+        cells_f[at, :] = layer_norm(fresh)
 
     def ring_step(s, carry):
         owners = (owner_at(pos - s), owner_at(pos + s))
-        for part in range(2):
+        for turn in range(4):
             for way in range(2):
+                part = orders[way][turn]
                 ring_copy(way, s, part, owners[way]).wait_recv()
-                if part == way:
+                if turn < 2:
                     ring_copy(way, s + 1, part, owners[way]).start()
                 else:
 
@@ -235,43 +249,43 @@
                     def _():
                         ring_copy(way, s + 1, part, owners[way]).start()
 
-            tri_part(part, owners[0])
-            tri_part(part, owners[1])
+            for way in range(2):
+                tri_part(orders[way][turn], owners[way])
+        finish(owner_at(pos - s + 1))
+
+        @pl.when(s > 1)
+        def _():
+            finish(owner_at(pos + s - 1))
+
         return carry
 
     lax.fori_loop(1, half_ring, ring_step, 0)
+    finish(owner_at(pos - half_ring + 1))
+    finish(owner_at(pos + half_ring - 1))
     far = owner_at(pos + half_ring)
-    for part in range(2):
-        ring_copy(part, half_ring, part, far).wait_recv()
-        tri_part(part, far)
-
-    def part_wait(owner, carry):
-        for part in range(2):
-            part_copy(part, owner).wait_recv()
-        return carry
-
-    lax.fori_loop(0, rows_n, part_wait, 0)
+    for turn in range(2):
+        for way in range(2):
+            ring_copy(way, half_ring, orders[way][turn], far).wait_recv()
+            tri_part(orders[way][turn], far)
+    finish(far)
 
     bias_own[...] = jnp.zeros_like(bias_own)
+    bias_w = jnp.concatenate(
+        [w_bias[...].astype(F32).T, jnp.zeros((16 - HEADS, channels), F32)], axis=0
+    ).astype(BF16)
 
     def norm_step(i, carry):
-        at = pl.ds(i, full, stride=8)
-        summed = acc[at, :] + part_in[at, :]
-        tri_norm = layer_norm(summed).astype(BF16)
-        fresh = after[i] + gate[i] * mul(tri_norm, w_tri_out[...])
-        fresh = fresh.astype(BF16).astype(F32)
-        after[i] = fresh
-        norm = layer_norm(fresh)
+        norm = cells_f[pl.ds(i, full, stride=8), :]
         if padded > full:
             norm = jnp.concatenate([norm, jnp.zeros((padded - full, channels), F32)], axis=0)
         norm = norm.astype(BF16)
         slab[i] = norm
-        bias = mul_t(w_bias[...], norm)
+        bias = mul_t(bias_w, norm)
         for h in range(HEADS):
             bias_own[pl.ds(8 * h + i, 1), :] = bias[h : h + 1]
         return carry
 
-    lax.fori_loop(0, slab_rows, norm_step, 0)
+    loop(slab_rows, norm_step)
     bias_all[me] = bias_own[...].astype(BF16)
 
     def bias_copy(t):
@@ -304,16 +318,26 @@
 
     head_of = lax.broadcasted_iota(jnp.int32, (full, channels), 1) // head_size
 
+    def score(h, query, key):
+        query = jnp.where(head_of == h, query.astype(F32), 0.0).astype(BF16)
+        return mul_t(query, key)
+
     def att_step(i, carry):
         proj = mul(slab[i], w_att[...])
-        queries_s[i] = (proj[:full, :channels] * head_size ** (-0.5)).astype(BF16)
-        keys_s[i] = proj[:, channels : 2 * channels].astype(BF16)
+        query = (proj[:full, :channels] * head_size ** (-0.5)).astype(BF16)
+        key = proj[:, channels : 2 * channels].astype(BF16)
+        if early:
+            for h in range(HEADS):
+                scores_s[i * HEADS + h] = score(h, query, key)
+        else:
+            queries_s[i] = query
+            keys_s[i] = key
         values_s[i, :, :channels] = proj[:, 2 * channels : 3 * channels].astype(BF16)
         values_s[i, :, channels:] = jnp.ones((padded, channels), BF16)
         att_gate[i] = jax.nn.sigmoid(proj[:full, 3 * channels :])
         return carry
 
-    lax.fori_loop(0, slab_rows, att_step, 0)
+    loop(slab_rows, att_step)
 
     def bias_wait(t, carry):
         bias_arrival(t).wait_recv()
@@ -329,44 +353,47 @@
             )
 
     def row_step(i, carry):
-        query = queries_s[i].astype(F32)
-        key = keys_s[i]
         value = values_s[i]
         top = jnp.zeros((full, channels), F32)
         bottom = jnp.zeros((full, channels), F32)
         for h in range(HEADS):
             mine = head_of == h
-            scores = mul_t(jnp.where(mine, query, 0.0).astype(BF16), key) + bias_f[h]
+            if early:
+                scores = scores_s[i * HEADS + h] + bias_f[h]
+            else:
+                scores = score(h, queries_s[i], keys_s[i]) + bias_f[h]
             peak = jnp.max(scores, axis=-1, keepdims=True)
             expo = jnp.exp(scores - peak).astype(BF16)
             mixed = mul(expo, value)
             top = jnp.where(mine, mixed[:, :channels], top)
             bottom = jnp.where(mine, mixed[:, channels:], bottom)
         gated = (att_gate[i] * (top / bottom)).astype(BF16)
-        second = (after[i] + mul(gated, w_att_out[...])).astype(BF16).astype(F32)
+        second = (acc[pl.ds(i, full, stride=8), :] + mul(gated, w_att_out[...])).astype(BF16).astype(F32)
         hidden = mul(layer_norm(second).astype(BF16), w_up[...])
         activated = jax.nn.silu(hidden[:, :hidden_units]) * hidden[:, hidden_units:]
         result = second + mul(activated.astype(BF16), w_down[...])
-        out_ref[i] = result.astype(BF16)
-        return carry
-
-    lax.fori_loop(0, slab_rows, row_step, 0)
+        out_ref[i] = result
+        return carry
+
+    loop(slab_rows, row_step)
 
     pair_copy.wait_send()
 
     def ring_drain(s, carry):
         owners = (owner_at(pos - s), owner_at(pos + s))
         for way in range(2):
-            for part in range(2):
+            for part in range(4):
                 ring_copy(way, s + 1, part, owners[way]).wait_send()
         return carry
 
     lax.fori_loop(0, half_ring - 1, ring_drain, 0)
-    ring_copy(0, half_ring, 0, owner_at(pos - half_ring + 1)).wait_send()
-    ring_copy(1, half_ring, 1, owner_at(pos + half_ring - 1)).wait_send()
+    lasts = (owner_at(pos - half_ring + 1), owner_at(pos + half_ring - 1))
+    for way in range(2):
+        for turn in range(2):
+            ring_copy(way, half_ring, orders[way][turn], lasts[way]).wait_send()
 
     def part_drain(owner, carry):
-        for part in range(2):
+        for part in range(4):
             part_copy(part, owner).wait_send()
         return carry
 
@@ -386,12 +413,12 @@
     slab_rows = rows // 2
     peers = 2 * rows_n
     half_ring = rows_n // 2
-    bias_t = jnp.pad(w_bias.T, ((0, 16 - HEADS), (0, 0)))
+    kept = (slab_rows * HEADS, full, padded) if full <= 128 else (1, 8, 128)
     vmem = pl.BlockSpec(memory_space=pltpu.VMEM)
     dma = pltpu.SemaphoreType.DMA
-    return pl.pallas_call(
+    result = pl.pallas_call(
         functools.partial(kernel, rows_n),
-        out_shape=jax.ShapeDtypeStruct((slab_rows, full, channels), BF16),
+        out_shape=jax.ShapeDtypeStruct((slab_rows, full, channels), F32),
         in_specs=[pl.BlockSpec(memory_space=pltpu.SMEM)] + [vmem] * 8,
         out_specs=vmem,
         scratch_shapes=[
@@ -399,11 +426,12 @@
             pltpu.VMEM((rows_n * rows * cols, channels), BF16),
             pltpu.VMEM((rows, cols, channels), F32),
             pltpu.VMEM((slab_rows, cols, channels), BF16),
-            pltpu.VMEM((slab_rows, full, channels), F32),
             pltpu.VMEM((full * 8, channels), F32),
             pltpu.VMEM((full * 8, channels), F32),
             pltpu.VMEM((full * 8, channels), F32),
-            pltpu.VMEM((slab_rows, full, channels), F32),
+            pltpu.VMEM((full * 8, channels), F32),
+            pltpu.VMEM((full * 8, channels), F32),
+            pltpu.VMEM(kept, F32),
             pltpu.VMEM((slab_rows, padded, channels), BF16),
             pltpu.VMEM((slab_rows, padded, channels), BF16),
             pltpu.VMEM((slab_rows, padded, 2 * channels), BF16),
@@ -412,10 +440,10 @@
             pltpu.VMEM((HEADS * 8, padded), F32),
             pltpu.VMEM((peers, HEADS * 8, padded), BF16),
             pltpu.VMEM((HEADS, full, padded), F32),
-            dma((2, half_ring + 1, 2)),
-            dma((2, half_ring + 1, 2)),
-            dma((rows_n, 2)),
-            dma((rows_n, 2)),
+            dma((2, half_ring + 1, 4)),
+            dma((2, half_ring + 1, 4)),
+            dma((rows_n, 4)),
+            dma((rows_n, 4)),
             dma,
             dma,
             dma((peers,)),
@@ -424,7 +452,8 @@
         compiler_params=pltpu.CompilerParams(
             collective_id=0, has_side_effects=True, vmem_limit_bytes=60 * 2**20
         ),
-    )(length, pair, w_tri_in, w_tri_out, w_att, bias_t, w_att_out, w_up, w_down)
+    )(length, pair, w_tri_in, w_tri_out, w_att, w_bias, w_att_out, w_up, w_down)
+    return result.astype(BF16)
 
 
 def solution(mesh):

time: 50.3 us -> 42.1 us (0.84)
  Pallas kernels: 46.6 us -> 38.8 us
  local copies, waits for them, and re-layouts: 2.89 us -> 0.75 us
  other arithmetic: 0 us -> 1.7 us
    pallas_call x1, Pallas kernels: 46.6 us -> 38.8 us  [shards(): pl.pallas_call(functools.partial(kernel, rows_n), out_shape=jax.ShapeDtyp...]
    convert_element_type x0 -> x1, other arithmetic: none -> 1.7 us  [shards(): return result.astype(BF16)]
    unnamed x3, local copies, waits for them, and re-layouts: 2.29 us -> 0.75 us
    pad x1 -> x0, local copies, waits for them, and re-layouts: 0.6 us -> none  [shards(): bias_t = jnp.pad(w_bias.T, ((0, 16 - HEADS), (0, 0)))]
where the time goes in v2:
time: 42.1 us; the launch traced here: 41.9 us
  Pallas kernels  38.8 us (92%)
  other arithmetic  1.7 us (4%)
  local copies, waits for them, and re-layouts  0.75 us (2%)
  between operations  0.68 us (2%)
    pallas_call x1, Pallas kernels, shards(): pl.pallas_call(functools.partial(kernel, rows_n), out_shape=jax.ShapeDtyp...  38.8 us
    convert_element_type x1, other arithmetic, shards(): return result.astype(BF16)  1.7 us

profile of v2, /device:TPU:0, one launch (start us, length us, event | category | flops | bytes accessed | tf_op | source)
XLA Modules:
  0.0 41.9 jit_solution(537737907226995001)
XLA Ops:
  0.0 0.0 copy-start
  0.7 0.0 copy-done
  0.7 0.7 %copy.10.w_bias = bf16[128,4]{1,0:T(8,128)(2,1)} copy(bf16[128,4]{0,1:T(4,128)(2,1)S(1)} %copy-done) | data formatting | bytes 2048 | tf_op args[5]
  1.4 38.8 %shard_map.91 = f32[7,112,128]{2,1,0:T(8,128)} custom-call(s32[1]{0:T(128)S(6)} %copy.11.length_ref, bf16[14,56,128]{2,1,0:T(8,128)(2,1)} %pair_ref.1, bf16[128,640]{1,0:T(8,128)(2,1)} %w_tri_in.1, bf16[128,128]{1,0:T(8,128)(2,1)} %w_tri_out.1, bf16[128,512]{1,0:T(8,128)(2,1)} %w_att.1, bf16[128,4]{1,0:T(8,128)(2,1)} %copy.10.w_bias, ...), custom_call_target="tpu_custom_call" | custom-call | tf_op jit(solution)/shard_map/pallas_call | solution.py:419
  40.2 1.7 %convert_element_type.3 = bf16[7,112,128]{2,1,0:T(8,128)(2,1)} convert(f32[7,112,128]{2,1,0:T(8,128)} %shard_map.91) | non-fusion elementwise | flops 100352 | bytes 602112 | tf_op jit(solution)/shard_map/convert_element_type | solution.py:456
Async XLA Ops:
  0.0 0.7 %copy-start = (bf16[128,4]{0,1:T(4,128)(2,1)S(1)}, bf16[128,4]{0,1:T(4,128)(2,1)}, u32[]{:S(2)}) copy-start(bf16[128,4]{0,1:T(4,128)(2,1)} %param.14) | copy-start | bytes 3076

commit v3 on v2

--- a/solution.py
+++ b/solution.py
@@ -30,6 +30,16 @@
 
 def kernel(
     rows_n,
+    length_hbm,
+    pair_hbm,
+    w_tri_in_hbm,
+    w_tri_out_hbm,
+    w_att_hbm,
+    w_bias_hbm,
+    w_att_out_hbm,
+    w_up_hbm,
+    w_down_hbm,
+    out_ref,
     length_ref,
     pair_ref,
     w_tri_in,
@@ -39,7 +49,7 @@
     w_att_out,
     w_up,
     w_down,
-    out_ref,
+    load_sem,
     normed,
     right_all,
     left_f,
@@ -113,6 +123,24 @@
         )
     pl.semaphore_signal(barrier, inc=1, device_id={"col": 1 - col}, device_id_type=MESH)
 
+    operands = (
+        (length_hbm, length_ref),
+        (pair_hbm, pair_ref),
+        (w_tri_in_hbm, w_tri_in),
+        (w_tri_out_hbm, w_tri_out),
+        (w_bias_hbm, w_bias),
+        (w_att_hbm, w_att),
+        (w_att_out_hbm, w_att_out),
+        (w_up_hbm, w_up),
+        (w_down_hbm, w_down),
+    )
+    loads = [
+        pltpu.make_async_copy(src, dst, load_sem.at[k]) for k, (src, dst) in enumerate(operands)
+    ]
+    for load in loads:
+        load.start()
+    for load in loads[:3]:
+        load.wait()
     length = length_ref[0]
     row_off = row * rows
     col_off = col * cols
@@ -224,6 +252,7 @@
         return carry
 
     lax.fori_loop(0, slab_rows, gate_step, 0)
+    loads[3].wait()
 
     def finish(owner):
         for part in range(4):
@@ -268,10 +297,12 @@
             ring_copy(way, half_ring, orders[way][turn], far).wait_recv()
             tri_part(orders[way][turn], far)
     finish(far)
+    for load in loads[4:]:
+        load.wait()
 
     bias_own[...] = jnp.zeros_like(bias_own)
     bias_w = jnp.concatenate(
-        [w_bias[...].astype(F32).T, jnp.zeros((16 - HEADS, channels), F32)], axis=0
+        [w_bias[...].astype(F32), jnp.zeros((16 - HEADS, channels), F32)], axis=0
     ).astype(BF16)
 
     def norm_step(i, carry):
@@ -416,12 +447,16 @@
     kept = (slab_rows * HEADS, full, padded) if full <= 128 else (1, 8, 128)
     vmem = pl.BlockSpec(memory_space=pltpu.VMEM)
     dma = pltpu.SemaphoreType.DMA
+    operands = (pair, w_tri_in, w_tri_out, w_att, w_bias.T, w_att_out, w_up, w_down)
     result = pl.pallas_call(
         functools.partial(kernel, rows_n),
         out_shape=jax.ShapeDtypeStruct((slab_rows, full, channels), F32),
-        in_specs=[pl.BlockSpec(memory_space=pltpu.SMEM)] + [vmem] * 8,
+        in_specs=[pl.BlockSpec(memory_space=pl.ANY)] * 9,
         out_specs=vmem,
         scratch_shapes=[
+            pltpu.SMEM(length.shape, jnp.int32),
+            *(pltpu.VMEM(operand.shape, BF16) for operand in operands),
+            dma((9,)),
             pltpu.VMEM((rows * cols, channels), BF16),
             pltpu.VMEM((rows_n * rows * cols, channels), BF16),
             pltpu.VMEM((rows, cols, channels), F32),
@@ -452,7 +487,7 @@
         compiler_params=pltpu.CompilerParams(
             collective_id=0, has_side_effects=True, vmem_limit_bytes=60 * 2**20
         ),
-    )(length, pair, w_tri_in, w_tri_out, w_att, w_bias, w_att_out, w_up, w_down)
+    )(length, *operands)
     return result.astype(BF16)
 
 

time: 42.1 us -> 41.2 us (0.979)
  local copies, waits for them, and re-layouts: 0.75 us -> 0 us
    unnamed x3 -> x0, local copies, waits for them, and re-layouts: 0.75 us -> none
where the time goes in v3:
time: 41.2 us; the launch traced here: 41 us
  Pallas kernels  38.7 us (94%)
  other arithmetic  1.7 us (4%)
  between operations  0.66 us (2%)
    pallas_call x1, Pallas kernels, shards(): pl.pallas_call(functools.partial(kernel, rows_n), out_shape=jax.ShapeDtyp...  38.7 us
    convert_element_type x1, other arithmetic, shards(): return result.astype(BF16)  1.7 us

profile of v3, /device:TPU:0, one launch (start us, length us, event | category | flops | bytes accessed | tf_op | source)
XLA Modules:
  0.0 41.0 jit_solution(2684624520908192839)
XLA Ops:
  0.7 38.7 %shard_map.91 = f32[7,112,128]{2,1,0:T(8,128)} custom-call(s32[1]{0:T(128)S(6)} %copy.10.length_hbm, bf16[14,56,128]{2,1,0:T(8,128)(2,1)} %pair_hbm.1, bf16[128,640]{1,0:T(8,128)(2,1)} %w_tri_in_hbm.1, bf16[128,128]{1,0:T(8,128)(2,1)} %w_tri_out_hbm.1, bf16[128,512]{1,0:T(8,128)(2,1)} %w_att_hbm.1, bf16[4,128]{1,0:T(4,128)(2,1)} %bitcast.1, ...), custom_call_target="tpu_custom_call" | custom-call | tf_op jit(solution)/shard_map/pallas_call | solution.py:451
  39.3 1.7 %convert_element_type.3 = bf16[7,112,128]{2,1,0:T(8,128)(2,1)} convert(f32[7,112,128]{2,1,0:T(8,128)} %shard_map.91) | non-fusion elementwise | flops 100352 | bytes 602112 | tf_op jit(solution)/shard_map/convert_element_type | solution.py:491

commit v4 on v3

--- a/solution.py
+++ b/solution.py
@@ -319,33 +319,33 @@
     loop(slab_rows, norm_step)
     bias_all[me] = bias_own[...].astype(BF16)
 
-    def bias_copy(t):
-        peer = lax.rem(me + t, peers)
+    def bias_move(slot, sem, peer):
         return pltpu.make_async_remote_copy(
-            src_ref=bias_all.at[me],
-            dst_ref=bias_all.at[me],
-            send_sem=bias_send.at[t],
-            recv_sem=bias_recv.at[t],
-            device_id={"row": peer // 2, "col": peer % 2},
+            src_ref=bias_all.at[slot],
+            dst_ref=bias_all.at[slot],
+            send_sem=bias_send.at[sem],
+            recv_sem=bias_recv.at[sem],
+            device_id=peer,
             device_id_type=MESH,
         )
 
+    def bias_copy(t):
+        return bias_move(me, t, {"row": lax.rem(row + t, rows_n)})
+
     def bias_arrival(t):
-        peer = lax.rem(me + peers - t, peers)
-        return pltpu.make_async_remote_copy(
-            src_ref=bias_all.at[peer],
-            dst_ref=bias_all.at[peer],
-            send_sem=bias_send.at[t],
-            recv_sem=bias_recv.at[t],
-            device_id={"row": peer // 2, "col": peer % 2},
-            device_id_type=MESH,
-        )
+        source = lax.rem(row + rows_n - t, rows_n)
+        return bias_move(source * 2 + col, t, {"row": source})
+
+    def bias_share(t, core):
+        source = lax.rem(row + rows_n - t, rows_n)
+        return bias_move(source * 2 + core, rows_n + t, {"col": 1 - col})
 
     def bias_start(t, carry):
         bias_copy(t).start()
         return carry
 
-    lax.fori_loop(1, peers, bias_start, 0)
+    lax.fori_loop(1, rows_n, bias_start, 0)
+    bias_share(0, col).start()
 
     head_of = lax.broadcasted_iota(jnp.int32, (full, channels), 1) // head_size
 
@@ -370,11 +370,17 @@
 
     loop(slab_rows, att_step)
 
+    def bias_pass(t, carry):
+        bias_arrival(t).wait_recv()
+        bias_share(t, col).start()
+        return carry
+
     def bias_wait(t, carry):
-        bias_arrival(t).wait_recv()
-        return carry
-
-    lax.fori_loop(1, peers, bias_wait, 0)
+        bias_share(t, 1 - col).wait_recv()
+        return carry
+
+    lax.fori_loop(1, rows_n, bias_pass, 0)
+    lax.fori_loop(0, rows_n, bias_wait, 0)
     key_ok = lax.broadcasted_iota(jnp.int32, (slab_rows, padded), 1) < length
     for peer in range(peers):
         block = bias_all[peer].astype(F32)
@@ -432,9 +438,11 @@
 
     def bias_drain(t, carry):
         bias_copy(t).wait_send()
-        return carry
-
-    lax.fori_loop(1, peers, bias_drain, 0)
+        bias_share(t, col).wait_send()
+        return carry
+
+    bias_share(0, col).wait_send()
+    lax.fori_loop(1, rows_n, bias_drain, 0)
 
 
 def shards(rows_n, pair, length, w_tri_in, w_tri_out, w_att, w_bias, w_att_out, w_up, w_down):

time: 41.2 us -> 41 us (level); the launches traced: 41 us -> 40.2 us
  Pallas kernels: 38.7 us -> 37.9 us
    pallas_call x1, Pallas kernels: 38.7 us -> 37.9 us  [shards(): pl.pallas_call(functools.partial(kernel, rows_n), out_shape=jax.ShapeDtyp...]
where the time goes in v4:
time: 41 us; the launch traced here: 40.2 us
  Pallas kernels  37.9 us (92%)
  other arithmetic  1.7 us (4%)
  between operations  0.66 us (2%)
    pallas_call x1, Pallas kernels, shards(): pl.pallas_call(functools.partial(kernel, rows_n), out_shape=jax.ShapeDtyp...  37.9 us
    convert_element_type x1, other arithmetic, shards(): return result.astype(BF16)  1.7 us

profile of v4, /device:TPU:0, one launch (start us, length us, event | category | flops | bytes accessed | tf_op | source)
XLA Modules:
  0.0 40.2 jit_solution(15659080449438184609)
XLA Ops:
  0.7 37.9 %shard_map.91 = f32[7,112,128]{2,1,0:T(8,128)} custom-call(s32[1]{0:T(128)S(6)} %copy.10.length_hbm, bf16[14,56,128]{2,1,0:T(8,128)(2,1)} %pair_hbm.1, bf16[128,640]{1,0:T(8,128)(2,1)} %w_tri_in_hbm.1, bf16[128,128]{1,0:T(8,128)(2,1)} %w_tri_out_hbm.1, bf16[128,512]{1,0:T(8,128)(2,1)} %w_att_hbm.1, bf16[4,128]{1,0:T(4,128)(2,1)} %bitcast.1, ...), custom_call_target="tpu_custom_call" | custom-call | tf_op jit(solution)/shard_map/pallas_call | solution.py:459
  38.5 1.7 %convert_element_type.3 = bf16[7,112,128]{2,1,0:T(8,128)(2,1)} convert(f32[7,112,128]{2,1,0:T(8,128)} %shard_map.91) | non-fusion elementwise | flops 100352 | bytes 602112 | tf_op jit(solution)/shard_map/convert_element_type | solution.py:499
